TPU v7x, 32 devices: a whole 2x2x4 slice. The times are simulated.
32 devices in a mesh: space: 16 (over z, y, x), sens: 2 (over core).
Axes of the slice: x: 2, y: 2, z: 4, core: 2. Of those that a mesh axis runs over, the one named last changes fastest.
Arguments:
- adjoint_end: float32 [16, 64, 64, 128], P('sens', 'space'), may hold values from -6 to 6
- checkpoints: float32 [8, 64, 64, 128], P('sens', 'space'), may hold values from 0.5 to 2
- dispersion: float32 [6, 64, 64, 128], P(None, 'space', 'sens'), as said below
- owner_steps: int32 [3], replicated, may hold values from 0 to 7, as said below
- sensor_cells: int32 [16], P('sens'), may hold values from 0 to 524287
- misfit: float32 [16, 3], P('sens'), may hold values from -6 to 6
- release_cells: int32 [128], replicated, may hold values from 0 to 524287
- release_steps: int32 [128], replicated, may hold values from 0 to 2
Outputs:
- adjoint: float32 [16, 64, 64, 128], P('sens', 'space')
- release_grad: float32 [16, 128], P('sens')
Inputs may be any that keep to these rules, and one draw needn't show every extreme that they name: `owner_steps`: the entries are different stored states; the first and the last stored state are always among them. `sensor_cells`: flat cell indices. `release_cells`: flat cell indices. `dispersion`: zz, yy and xx components are positive.
All inputs are finite; a program needn't handle non-finite values.
Results may differ from a plain program's by a relative error of at most 0.00002.
Values sent between devices are 32-bit elements; how exact they have to be, the bound alone decides.
No kernel may reach another device: no remote copies, remote signals or barrier semaphores. Data moves between devices by JAX's collectives and lax.ppermute only.
A program may use at most 128 MiB of HBM per device.

v0:
```python
import jax
import jax.numpy as jnp
from jax import lax
from jax.sharding import PartitionSpec as P

STEPS = 3
step_dt = 0.12


def extended(block, sides, width):
    for axis, dim in sides:
        count = lax.axis_size(axis)
        forward = [(i, i + 1) for i in range(count - 1)]
        backward = [(target, source) for source, target in forward]
        low = lax.ppermute(
            lax.slice_in_dim(block, block.shape[dim] - width, None, axis=dim), axis, forward
        )
        high = lax.ppermute(lax.slice_in_dim(block, 0, width, axis=dim), axis, backward)
        block = jnp.concatenate([low, block, high], axis=dim)
    return block


def broadcast(array, axis, root):
    mine = lax.axis_index(axis) == root
    return lax.psum(jnp.where(mine, array, jnp.zeros_like(array)), axis)


def retard_scale(conc):
    return step_dt / (1.0 + 0.5 * conc ** (-0.5))


def retard_slope(conc):
    retard = 1.0 + 0.5 * conc ** (-0.5)
    deriv = -0.25 * conc ** (-1.5)
    return -step_dt * deriv / (retard * retard)


def apply_op(field, tensor):
    depth = field.shape[1] - 2
    rows_y = field.shape[2]
    rows_x = field.shape[3]
    padded = jnp.pad(field, ((0, 0), (0, 0), (1, 1), (1, 1)))
    coeffs = jnp.pad(tensor, ((0, 0), (0, 0), (1, 1), (1, 1)))

    def at_shift(arr, shift):
        return arr[
            ...,
            1 + shift[0] : 1 + shift[0] + depth,
            1 + shift[1] : 1 + shift[1] + rows_y,
            1 + shift[2] : 1 + shift[2] + rows_x,
        ]

    units = [(1, 0, 0), (0, 1, 0), (0, 0, 1)]
    centre = (0, 0, 0)
    total = jnp.zeros((field.shape[0], depth, rows_y, rows_x), jnp.float32)
    for axis_id in range(3):
        plus = units[axis_id]
        minus = tuple((-v for v in plus))
        diag = coeffs[axis_id]
        a_plus = 0.5 * (at_shift(diag, centre) + at_shift(diag, plus))
        a_minus = 0.5 * (at_shift(diag, centre) + at_shift(diag, minus))
        total = total + a_plus * (at_shift(padded, plus) - at_shift(padded, centre))
        total = total - a_minus * (at_shift(padded, centre) - at_shift(padded, minus))
    for first, second, comp in ((0, 1, 3), (0, 2, 4), (1, 2, 5)):
        for outer, inner in ((first, second), (second, first)):
            unit_o = units[outer]
            unit_i = units[inner]
            for sign in (1, -1):
                spot = tuple((sign * v for v in unit_o))
                up_spot = tuple((spot[t] + unit_i[t] for t in range(3)))
                down_spot = tuple((spot[t] - unit_i[t] for t in range(3)))
                flux = at_shift(coeffs[comp], spot) * (
                    0.5 * (at_shift(padded, up_spot) - at_shift(padded, down_spot))
                )
                total = total + 0.5 * sign * flux
    return total


def add_misfit(field, column, sensor_cells, start_cell):
    count = field.shape[0]
    cells = field.shape[1] * field.shape[2] * field.shape[3]
    local = sensor_cells - start_cell
    positions = lax.broadcasted_iota(jnp.int32, (count, cells), 1)
    hit = positions == local[:, None]
    return field + jnp.where(hit, column[:, None], 0.0).reshape(field.shape)


def body(
    adjoint_end,
    checkpoints,
    dispersion,
    owner_steps,
    sensor_cells,
    misfit,
    release_cells,
    release_steps,
):
    own_sensors, depth, rows_y, rows_x = adjoint_end.shape
    slot_count = checkpoints.shape[0]
    cells = depth * rows_y * rows_x
    first_cell = lax.axis_index("space") * cells
    release_local = release_cells - first_cell
    release_inside = (release_local >= 0) & (release_local < cells)
    release_index = jnp.clip(release_local, 0, cells - 1)
    lam = adjoint_end
    partial_grad = jnp.zeros((own_sensors, release_cells.shape[0]), jnp.float32)
    whole = lax.all_gather(dispersion, "sens", axis=2, tiled=True)
    tensor = extended(whole, (("space", 1),), 1)
    for step in reversed(range(STEPS)):
        holder = owner_steps[step] // slot_count
        mine = lax.dynamic_index_in_dim(
            checkpoints, owner_steps[step] % slot_count, 0, keepdims=False
        )
        conc = broadcast(mine, "sens", holder)
        mixed = add_misfit(lam, misfit[:, step], sensor_cells, first_cell)
        scaled = retard_scale(conc) * mixed
        stacked = jnp.concatenate([conc[None], scaled], 0)
        rimmed = extended(stacked, (("space", 1),), 1)
        applied = apply_op(rimmed, tensor)
        lam = mixed + applied[1:] + retard_slope(conc) * applied[0] * mixed
        values = jnp.take(lam.reshape(own_sensors, cells), release_index, axis=1)
        keep = release_inside & (release_steps == step)
        partial_grad = partial_grad + jnp.where(keep[None, :], values, 0.0)
    release_grad = lax.psum(partial_grad, "space")
    return (lam, release_grad)


def solution(mesh):
    in_specs = (
        P("sens", "space", None, None),
        P("sens", "space", None, None),
        P(None, "space", "sens", None),
        P(),
        P("sens"),
        P("sens", None),
        P(),
        P(),
    )
    out_specs = (P("sens", "space", None, None), P("sens", None))
    return jax.shard_map(body, mesh=mesh, in_specs=in_specs, out_specs=out_specs, check_vma=False)
```

profile of v0, /device:TPU:0, one launch (start us, length us, event | category | flops | bytes accessed | tf_op | source)
XLA Modules:
  0.0 248.9 jit_solution(358271755512530131)
XLA Ops:
  7.2 0.0 all-reduce.7.cloned.1.call-start
  7.2 2.8 %all_gather.3 = f32[6,4,64,128]{3,2,1,0:T(8,128)S(1)} all-gather(f32[6,4,32,128]{3,2,1,0:T(8,128)} %param.12), channel_id=1, replica_groups=mesh['space'=16,'sens'=2] {'sens'}, dimensions={2}, use_global_device_ids=true | all-gather | bytes 1179648 | tf_op jit(solution)/shard_map/all_gather | solution.py:107
  10.1 4.8 %collective-permute-start = (f32[6,1,64,128]{3,2,1,0:T(8,128)S(1)}, f32[6,1,64,128]{3,2,1,0:T(8,128)S(1)}, u32[]{:S(2)}, u32[]{:S(2)}) collective-permute-start(f32[6,1,64,128]{3,2,1,0:T(8,128)S(1)} %get-tuple-element.28), channel_id=1, source_target_pairs={{0,2},{2,4},{4,6},{6,8},{8,10},{10,12},{12,14},{14,16},{16,18},{18... | collective-permute-start | bytes 589832 | tf_op jit(solution)/shard_map/ppermute | solution.py:15
  14.8 1.3 collective-permute-start.1
  16.2 0.6 fusion.113
  24.6 0.8 select_bitcast_fusion
  25.3 0.0 all-reduce.7.cloned.1.call-update
  25.4 0.0 copy-done.58
  25.4 0.0 collective-permute-done
  25.4 0.0 collective-permute-done.1
  25.5 0.8 select_maximum_fusion.9
  26.2 1.2 slice_bitcast_fusion.5
  27.4 1.0 slice_multiply_fusion.11
  28.5 0.3 slice_multiply_fusion.3
  28.8 17.7 %all-reduce.7.cloned.1.call-done = (f32[4,64,128]{2,1,0:T(8,128)}, f32[4,64,128]{2,1,0:T(8,128)}, f32[4,64,128]{2,1,0:T(8,128)}) async-done(((f32[4,64,128]{2,1,0:T(8,128)}, f32[4,64,128]{2,1,0:T(8,128)}, f32[4,64,128]{2,1,0:T(8,128)}), (f32[4,64,128]{2,1,0:T(8,128)}, f32[4,64,128]{2,1,0:T(8,128)}, f32[4,64,128]{2,1,0:T(8,128)})) %all-reduce.7.cloned.1.call-update) | async-done | bytes 393232 | tf_op jit(solution)/shard_map/psum | solution.py:25
  46.5 1.0 fusion.107
  47.5 0.3 fusion.89
  47.8 0.0 copy-start.48
  47.8 0.6 copy-done.4
  48.4 3.7 %collective-permute-start.3 = (f32[9,1,64,128]{3,2,1,0:T(8,128)S(1)}, f32[9,1,64,128]{3,2,1,0:T(8,128)S(1)}, u32[]{:S(2)}, u32[]{:S(2)}) collective-permute-start(f32[9,1,64,128]{3,2,1,0:T(8,128)S(1)} %get-tuple-element.26), channel_id=1, source_target_pairs={{0,2},{2,4},{4,6},{6,8},{8,10},{10,12},{12,14},{14,16},{16,18},{18... | collective-permute-start | bytes 884744 | tf_op jit(solution)/shard_map/ppermute | solution.py:15
  52.1 1.3 collective-permute-start.2
  53.4 0.0 copy-done.48
  53.4 0.0 copy-done.49
  53.5 0.3 fusion.102
  53.8 0.1 fusion.106
  53.9 11.3 %collective-permute-done.3 = f32[9,1,64,128]{3,2,1,0:T(8,128)S(1)} collective-permute-done((f32[9,1,64,128]{3,2,1,0:T(8,128)S(1)}, f32[9,1,64,128]{3,2,1,0:T(8,128)S(1)}, u32[]{:S(2)}, u32[]{:S(2)}) %collective-permute-start.3) | collective-permute-done | bytes 294944 | tf_op jit(solution)/shard_map/ppermute | solution.py:15
  65.1 1.9 collective-permute-done.2
  67.1 2.7 %select_maximum_fusion.6 = f32[9,6,66,130]{3,2,1,0:T(8,128)S(1)} fusion(f32[9,1,64,128]{3,2,1,0:T(8,128)S(1)} %collective-permute-done.2, f32[9,1,64,128]{3,2,1,0:T(8,128)S(1)} %collective-permute-done.3, f32[8,4,64,128]{3,2,1,0:T(8,128)S(1)} %fusion.89, f32[1,4,64,128]{3,2,1,0:T(8,128)S(1)} %bitcast.69), kind=kLoop, calls=%fused_computation.13 | loop fusion | flops 8339760 | bytes 3622752 | tf_op jit(solution)/shard_map/concatenate | solution.py:19
  69.9 4.7 %fusion.69 = f32[9,4,64,128]{3,2,1,0:T(8,128)S(1)} fusion(f32[9,6,66,130]{3,2,1,0:T(8,128)S(1)} %select_maximum_fusion.6, f32[9,1,64,128]{3,2,1,0:T(8,128)S(1)} %collective-permute-done.3, f32[8,4,64,128]{3,2,1,0:T(8,128)S(1)} %fusion.89, f32[1,4,64,128]{3,2,1,0:T(8,128)S(1)} %bitcast.70, f32[9,1,64,128]{3,2,1,0:T(8,128)S(1)} %collective-permute-done.2, ...), kind=kLoop, calls=%fused_computation.120 | loop fusion | flops 20643840 | bytes 24182784 | tf_op jit(solution)/shard_map/add | solution.py:75
  74.5 0.1 fusion.98
  74.6 0.6 fusion.88
  75.2 0.0 copy-start.57
  75.2 0.0 copy-start.59
  75.3 3.4 %collective-permute-start.5 = (f32[9,1,64,128]{3,2,1,0:T(8,128)S(1)}, f32[9,1,64,128]{3,2,1,0:T(8,128)S(1)}, u32[]{:S(2)}, u32[]{:S(2)}) collective-permute-start(f32[9,1,64,128]{3,2,1,0:T(8,128)S(1)} %get-tuple-element.24), channel_id=1, source_target_pairs={{0,2},{2,4},{4,6},{6,8},{8,10},{10,12},{12,14},{14,16},{16,18},{18... | collective-permute-start | bytes 884744 | tf_op jit(solution)/shard_map/ppermute | solution.py:15
  78.7 1.5 collective-permute-start.4
  80.2 0.6 compare_and_fusion.3
  80.8 0.1 fusion.105
  80.9 10.0 %collective-permute-done.5 = f32[9,1,64,128]{3,2,1,0:T(8,128)S(1)} collective-permute-done((f32[9,1,64,128]{3,2,1,0:T(8,128)S(1)}, f32[9,1,64,128]{3,2,1,0:T(8,128)S(1)}, u32[]{:S(2)}, u32[]{:S(2)}) %collective-permute-start.5) | collective-permute-done | bytes 294944 | tf_op jit(solution)/shard_map/ppermute | solution.py:15
  90.9 0.7 collective-permute-done.4
  91.6 2.7 %select_maximum_fusion.3 = f32[9,6,66,130]{3,2,1,0:T(8,128)S(1)} fusion(f32[9,1,64,128]{3,2,1,0:T(8,128)S(1)} %collective-permute-done.4, f32[9,1,64,128]{3,2,1,0:T(8,128)S(1)} %collective-permute-done.5, f32[8,4,64,128]{3,2,1,0:T(8,128)S(1)} %get-tuple-element.14, f32[1,4,64,128]{3,2,1,0:T(8,128)S(1)} %bitcast.66), kind=kLoop, calls=%fused_computation.10 | loop fusion | flops 8339760 | bytes 3622752 | tf_op jit(solution)/shard_map/concatenate | solution.py:19
  94.4 4.7 %fusion.44 = f32[9,4,64,128]{3,2,1,0:T(8,128)S(1)} fusion(f32[9,6,66,130]{3,2,1,0:T(8,128)S(1)} %select_maximum_fusion.3, f32[9,1,64,128]{3,2,1,0:T(8,128)S(1)} %collective-permute-done.5, f32[8,4,64,128]{3,2,1,0:T(8,128)S(1)} %get-tuple-element.14, f32[1,4,64,128]{3,2,1,0:T(8,128)S(1)} %bitcast.67, f32[9,1,64,128]{3,2,1,0:T(8,128)S(1)} %collective-permute-done.4, ...), kind=kLoop, calls=%fused_computation.87 | loop fusion | flops 20643840 | bytes 24182784 | tf_op jit(solution)/shard_map/add | solution.py:75
  99.1 0.1 fusion.97
  99.2 0.6 fusion.87
  99.8 0.8 fusion.91
  100.6 4.3 %collective-permute-start.7 = (f32[9,1,64,128]{3,2,1,0:T(8,128)}, f32[9,1,64,128]{3,2,1,0:T(8,128)}, u32[]{:S(2)}, u32[]{:S(2)}) collective-permute-start(f32[9,1,64,128]{3,2,1,0:T(8,128)} %get-tuple-element.22), channel_id=1, source_target_pairs={{0,2},{2,4},{4,6},{6,8},{8,10},{10,12},{12,14},{14,16},{16,18},{18... | collective-permute-start | bytes 884744 | tf_op jit(solution)/shard_map/ppermute | solution.py:15
  105.0 1.3 collective-permute-start.6
  106.3 0.5 compare_and_fusion.2
  106.8 8.7 %copy.10 = f32[8,4,64,128]{0,3,2,1:T(8,128)} copy(f32[8,4,64,128]{3,2,1,0:T(8,128)S(1)} %get-tuple-element.15) | data formatting | bytes 2097152 | tf_op jit(solution)/shard_map/add | solution.py:120
  115.5 7.0 %gather_fusion = f32[128,8]{1,0:T(8,128)} fusion(f32[8,32768]{0,1:T(8,128)} %bitcast.59, s32[1024]{0:T(1024)S(1)} %pad_clamp_fusion), kind=kCustom, calls=%fused_computation.clone | custom fusion | bytes 8704 | tf_op jit(solution)/shard_map/jit(_take)/gather | solution.py:121
  122.5 8.7 %copy.11 = f32[8,4,64,128]{0,3,2,1:T(8,128)} copy(f32[8,4,64,128]{3,2,1,0:T(8,128)S(1)} %get-tuple-element.13) | data formatting | bytes 2097152 | tf_op jit(solution)/shard_map/add | solution.py:120
  131.1 7.0 %gather_fusion.1 = f32[128,8]{1,0:T(8,128)} fusion(f32[8,32768]{0,1:T(8,128)} %bitcast.61, s32[1024]{0:T(1024)S(1)} %pad_clamp_fusion), kind=kCustom, calls=%fused_computation.1.clone | custom fusion | bytes 8704 | tf_op jit(solution)/shard_map/jit(_take)/gather | solution.py:121
  138.3 0.0 collective-permute-done.7
  138.3 0.0 collective-permute-done.6
  138.3 3.9 %select_maximum_fusion = f32[9,6,66,130]{3,2,1,0:T(8,128)S(1)} fusion(f32[9,1,64,128]{3,2,1,0:T(8,128)} %collective-permute-done.6, f32[9,1,64,128]{3,2,1,0:T(8,128)} %collective-permute-done.7, f32[8,4,64,128]{3,2,1,0:T(8,128)S(1)} %get-tuple-element.12, f32[1,4,64,128]{3,2,1,0:T(8,128)S(1)} %bitcast.63), kind=kLoop, calls=%fused_computation.7 | loop fusion | flops 8339760 | bytes 3622752 | tf_op jit(solution)/shard_map/concatenate | solution.py:19
  142.4 5.7 %fusion.19 = f32[9,4,64,128]{3,2,1,0:T(8,128)S(1)} fusion(f32[9,6,66,130]{3,2,1,0:T(8,128)S(1)} %select_maximum_fusion, f32[9,1,64,128]{3,2,1,0:T(8,128)} %collective-permute-done.7, f32[8,4,64,128]{3,2,1,0:T(8,128)S(1)} %get-tuple-element.12, f32[1,4,64,128]{3,2,1,0:T(8,128)S(1)} %bitcast.64, f32[9,1,64,128]{3,2,1,0:T(8,128)} %collective-permute-done.6, ...), kind=kLoop, calls=%fused_computation.54 | loop fusion | flops 20643840 | bytes 24182784 | tf_op jit(solution)/shard_map/add | solution.py:75
  148.1 0.1 fusion.96
  148.2 0.4 fusion.84
  148.6 0.0 copy-start
  148.6 0.0 copy-start.54
  148.6 8.7 %copy.12 = f32[8,4,64,128]{0,3,2,1:T(8,128)} copy(f32[8,4,64,128]{3,2,1,0:T(8,128)S(1)} %fusion.84) | data formatting | bytes 2097152 | tf_op jit(solution)/shard_map/add | solution.py:120
  157.4 6.4 %gather_fusion.2 = f32[128,8]{1,0:T(8,128)S(1)} fusion(f32[8,32768]{0,1:T(8,128)} %bitcast.60, s32[1024]{0:T(1024)S(1)} %pad_clamp_fusion), kind=kCustom, calls=%fused_computation.2.clone | custom fusion | bytes 8704 | tf_op jit(solution)/shard_map/jit(_take)/gather | solution.py:121
  163.8 0.1 fusion.108
  164.0 77.5 %psum.31 = f32[8,128]{0,1:T(8,128)S(1)} all-reduce(f32[8,128]{0,1:T(8,128)S(1)} %fusion.108), channel_id=1, replica_groups=mesh['space'=16,'sens'=2] {'space'}, use_global_device_ids=true, to_apply=%region_3.5 | all-reduce | flops 1024 | bytes 8192 | tf_op jit(solution)/shard_map/psum | solution.py:124
  241.4 0.7 copy.13
  (120 shorter events, 0.4 us)
Async XLA Ops:
  7.2 9.0 %copy-start.53 = (s32[3]{0:T(128)S(1)}, s32[3]{0:T(128)}, u32[]{:S(2)}) copy-start(s32[3]{0:T(128)} %param.13) | copy-start | bytes 40
  7.2 17.4 %copy-start.50 = (f32[4,4,64,128]{3,2,1,0:T(8,128)S(1)}, f32[4,4,64,128]{3,2,1,0:T(8,128)}, u32[]{:S(2)}) copy-start(f32[4,4,64,128]{3,2,1,0:T(8,128)} %param.11) | copy-start | bytes 1572868
  7.2 39.3 %all-reduce.7.cloned.1.call-start = ((), (), s32[]{:S(2)}) async-start(), calls=%async_computation | async-start | bytes 786432 | tf_op jit(solution)/shard_map/psum | solution.py:25
  10.0 15.4 %copy-start.58 = (f32[8,3]{0,1:T(4,128)S(1)}, f32[8,3]{0,1:T(4,128)}, u32[]{:S(2)}) copy-start(f32[8,3]{0,1:T(4,128)} %param.15) | copy-start | bytes 292
  10.0 15.4 %copy-start.60 = (s32[8]{0:T(128)S(1)}, s32[8]{0:T(128)}, u32[]{:S(2)}) copy-start(s32[8]{0:T(128)} %param.14) | copy-start | bytes 100
  10.1 15.4 %collective-permute-start = (f32[6,1,64,128]{3,2,1,0:T(8,128)S(1)}, f32[6,1,64,128]{3,2,1,0:T(8,128)S(1)}, u32[]{:S(2)}, u32[]{:S(2)}) collective-permute-start(f32[6,1,64,128]{3,2,1,0:T(8,128)S(1)} %get-tuple-element.28), channel_id=1, source_target_pairs={{0,2},{2,4},{4,6},{6,8},{8,10},{10,12},{12,14},{14,16},{16,18},{18... | collective-permute-start | bytes 589832 | tf_op jit(solution)/shard_map/ppermute | solution.py:15
  14.8 10.6 %collective-permute-start.1 = (f32[6,1,64,128]{3,2,1,0:T(8,128)S(1)}, f32[6,1,64,128]{3,2,1,0:T(8,128)S(1)}, u32[]{:S(2)}, u32[]{:S(2)}) collective-permute-start(f32[6,1,64,128]{3,2,1,0:T(8,128)S(1)} %get-tuple-element.29), channel_id=1, source_target_pairs={{2,0},{4,2},{6,4},{8,6},{10,8},{12,10},{14,12},{16,14},{18,16},{20... | collective-permute-start | bytes 589832 | tf_op jit(solution)/shard_map/ppermute | solution.py:18
  28.4 41.3 %copy-start.33 = (f32[4,64,128]{2,1,0:T(8,128)}, f32[4,64,128]{2,1,0:T(8,128)S(1)}, u32[]{:S(2)}) copy-start(f32[4,64,128]{2,1,0:T(8,128)S(1)} %get-tuple-element.39) | copy-start | bytes 393220
  28.5 41.3 %copy-start.36 = (f32[4,64,128]{2,1,0:T(8,128)}, f32[4,64,128]{2,1,0:T(8,128)S(1)}, u32[]{:S(2)}) copy-start(f32[4,64,128]{2,1,0:T(8,128)S(1)} %get-tuple-element.40) | copy-start | bytes 393220
  28.5 41.3 %copy-start.39 = (f32[4,64,128]{2,1,0:T(8,128)}, f32[4,64,128]{2,1,0:T(8,128)S(1)}, u32[]{:S(2)}) copy-start(f32[4,64,128]{2,1,0:T(8,128)S(1)} %get-tuple-element.41) | copy-start | bytes 393220
  28.5 19.0 %copy-start.1 = (f32[8,4,64,128]{3,2,1,0:T(8,128)S(1)}, f32[8,4,64,128]{3,2,1,0:T(8,128)}, u32[]{:S(2)}) copy-start(f32[8,4,64,128]{3,2,1,0:T(8,128)} %param.10) | copy-start | bytes 3145732
  28.7 41.0 %copy-start.7 = (f32[4,64,128]{2,1,0:T(8,128)}, f32[4,64,128]{2,1,0:T(8,128)S(1)}, u32[]{:S(2)}) copy-start(f32[4,64,128]{2,1,0:T(8,128)S(1)} %get-tuple-element.49) | copy-start | bytes 393220
  28.8 41.0 %copy-start.10 = (f32[4,64,128]{2,1,0:T(8,128)}, f32[4,64,128]{2,1,0:T(8,128)S(1)}, u32[]{:S(2)}) copy-start(f32[4,64,128]{2,1,0:T(8,128)S(1)} %get-tuple-element.50) | copy-start | bytes 393220
  28.8 41.0 %copy-start.13 = (f32[4,64,128]{2,1,0:T(8,128)}, f32[4,64,128]{2,1,0:T(8,128)S(1)}, u32[]{:S(2)}) copy-start(f32[4,64,128]{2,1,0:T(8,128)S(1)} %get-tuple-element.61) | copy-start | bytes 393220
  28.8 41.0 %copy-start.16 = (f32[4,64,128]{2,1,0:T(8,128)}, f32[4,64,128]{2,1,0:T(8,128)S(1)}, u32[]{:S(2)}) copy-start(f32[4,64,128]{2,1,0:T(8,128)S(1)} %get-tuple-element.62) | copy-start | bytes 393220
  28.8 41.0 %copy-start.19 = (f32[4,64,128]{2,1,0:T(8,128)}, f32[4,64,128]{2,1,0:T(8,128)S(1)}, u32[]{:S(2)}) copy-start(f32[4,64,128]{2,1,0:T(8,128)S(1)} %get-tuple-element.63) | copy-start | bytes 393220
  28.8 41.0 %copy-start.22 = (f32[4,64,128]{2,1,0:T(8,128)}, f32[4,64,128]{2,1,0:T(8,128)S(1)}, u32[]{:S(2)}) copy-start(f32[4,64,128]{2,1,0:T(8,128)S(1)} %get-tuple-element.64) | copy-start | bytes 393220
  28.8 65.5 %copy-start.5 = (f32[4,64,128]{2,1,0:T(8,128)}, f32[4,64,128]{2,1,0:T(8,128)S(1)}, u32[]{:S(2)}) copy-start(f32[4,64,128]{2,1,0:T(8,128)S(1)} %get-tuple-element.48) | copy-start | bytes 393220
  47.8 5.7 %copy-start.48 = (f32[6,66,130]{2,1,0:T(8,128)S(1)}, f32[6,66,130]{2,1,0:T(8,128)}, u32[]{:S(2)}) copy-start(f32[6,66,130]{2,1,0:T(8,128)} %get-tuple-element.16) | copy-start | bytes 617764
  47.8 5.7 %copy-start.49 = (f32[6,66,130]{2,1,0:T(8,128)S(1)}, f32[6,66,130]{2,1,0:T(8,128)}, u32[]{:S(2)}) copy-start(f32[6,66,130]{2,1,0:T(8,128)} %get-tuple-element.20) | copy-start | bytes 617764
  48.4 5.4 %copy-start.3 = (f32[4,64,128]{2,1,0:T(8,128)S(1)}, f32[4,64,128]{2,1,0:T(8,128)}, u32[]{:S(2)}) copy-start(f32[4,64,128]{2,1,0:T(8,128)} %get-tuple-element.6) | copy-start | bytes 393220
  48.4 16.7 %collective-permute-start.3 = (f32[9,1,64,128]{3,2,1,0:T(8,128)S(1)}, f32[9,1,64,128]{3,2,1,0:T(8,128)S(1)}, u32[]{:S(2)}, u32[]{:S(2)}) collective-permute-start(f32[9,1,64,128]{3,2,1,0:T(8,128)S(1)} %get-tuple-element.26), channel_id=1, source_target_pairs={{0,2},{2,4},{4,6},{6,8},{8,10},{10,12},{12,14},{14,16},{16,18},{18... | collective-permute-start | bytes 884744 | tf_op jit(solution)/shard_map/ppermute | solution.py:15
  52.1 14.9 %collective-permute-start.2 = (f32[9,1,64,128]{3,2,1,0:T(8,128)S(1)}, f32[9,1,64,128]{3,2,1,0:T(8,128)S(1)}, u32[]{:S(2)}, u32[]{:S(2)}) collective-permute-start(f32[9,1,64,128]{3,2,1,0:T(8,128)S(1)} %get-tuple-element.27), channel_id=1, source_target_pairs={{2,0},{4,2},{6,4},{8,6},{10,8},{12,10},{14,12},{16,14},{18,16},{20... | collective-permute-start | bytes 884744 | tf_op jit(solution)/shard_map/ppermute | solution.py:18
  53.7 40.6 %copy-start.25 = (f32[4,64,128]{2,1,0:T(8,128)}, f32[4,64,128]{2,1,0:T(8,128)S(1)}, u32[]{:S(2)}) copy-start(f32[4,64,128]{2,1,0:T(8,128)S(1)} %get-tuple-element.35) | copy-start | bytes 393220
  53.7 40.6 %copy-start.27 = (f32[4,64,128]{2,1,0:T(8,128)}, f32[4,64,128]{2,1,0:T(8,128)S(1)}, u32[]{:S(2)}) copy-start(f32[4,64,128]{2,1,0:T(8,128)S(1)} %get-tuple-element.36) | copy-start | bytes 393220
  53.8 40.6 %copy-start.29 = (f32[4,64,128]{2,1,0:T(8,128)}, f32[4,64,128]{2,1,0:T(8,128)S(1)}, u32[]{:S(2)}) copy-start(f32[4,64,128]{2,1,0:T(8,128)S(1)} %get-tuple-element.67) | copy-start | bytes 393220
  53.8 40.6 %copy-start.31 = (f32[4,64,128]{2,1,0:T(8,128)}, f32[4,64,128]{2,1,0:T(8,128)S(1)}, u32[]{:S(2)}) copy-start(f32[4,64,128]{2,1,0:T(8,128)S(1)} %get-tuple-element.68) | copy-start | bytes 393220
  53.9 16.0 %copy-start.42 = (f32[4,64,128]{2,1,0:T(8,128)S(1)}, f32[4,64,128]{2,1,0:T(8,128)}, u32[]{:S(2)}) copy-start(f32[4,64,128]{2,1,0:T(8,128)} %get-tuple-element.42) | copy-start | bytes 393220
  53.9 16.0 %copy-start.44 = (f32[4,64,128]{2,1,0:T(8,128)S(1)}, f32[4,64,128]{2,1,0:T(8,128)}, u32[]{:S(2)}) copy-start(f32[4,64,128]{2,1,0:T(8,128)} %get-tuple-element.65) | copy-start | bytes 393220
  53.9 16.0 %copy-start.46 = (f32[4,64,128]{2,1,0:T(8,128)S(1)}, f32[4,64,128]{2,1,0:T(8,128)}, u32[]{:S(2)}) copy-start(f32[4,64,128]{2,1,0:T(8,128)} %get-tuple-element.66) | copy-start | bytes 393220
  75.2 5.0 %copy-start.57 = (s32[128]{0:T(128)S(1)}, s32[128]{0:T(128)}, u32[]{:S(2)}) copy-start(s32[128]{0:T(128)} %param.17) | copy-start | bytes 1540
  75.2 5.0 %copy-start.59 = (s32[128]{0:T(128)S(1)}, s32[128]{0:T(128)}, u32[]{:S(2)}) copy-start(s32[128]{0:T(128)} %param.16) | copy-start | bytes 1540
  75.2 5.5 %copy-start.2 = (f32[4,64,128]{2,1,0:T(8,128)S(1)}, f32[4,64,128]{2,1,0:T(8,128)}, u32[]{:S(2)}) copy-start(f32[4,64,128]{2,1,0:T(8,128)} %get-tuple-element.7) | copy-start | bytes 393220
  75.3 15.6 %collective-permute-start.5 = (f32[9,1,64,128]{3,2,1,0:T(8,128)S(1)}, f32[9,1,64,128]{3,2,1,0:T(8,128)S(1)}, u32[]{:S(2)}, u32[]{:S(2)}) collective-permute-start(f32[9,1,64,128]{3,2,1,0:T(8,128)S(1)} %get-tuple-element.24), channel_id=1, source_target_pairs={{0,2},{2,4},{4,6},{6,8},{8,10},{10,12},{12,14},{14,16},{16,18},{18... | collective-permute-start | bytes 884744 | tf_op jit(solution)/shard_map/ppermute | solution.py:15
  78.7 12.9 %collective-permute-start.4 = (f32[9,1,64,128]{3,2,1,0:T(8,128)S(1)}, f32[9,1,64,128]{3,2,1,0:T(8,128)S(1)}, u32[]{:S(2)}, u32[]{:S(2)}) collective-permute-start(f32[9,1,64,128]{3,2,1,0:T(8,128)S(1)} %get-tuple-element.25), channel_id=1, source_target_pairs={{2,0},{4,2},{6,4},{8,6},{10,8},{12,10},{14,12},{16,14},{18,16},{20... | collective-permute-start | bytes 884744 | tf_op jit(solution)/shard_map/ppermute | solution.py:18
  80.8 13.5 %copy-start.8 = (f32[4,64,128]{2,1,0:T(8,128)S(1)}, f32[4,64,128]{2,1,0:T(8,128)}, u32[]{:S(2)}) copy-start(f32[4,64,128]{2,1,0:T(8,128)} %copy-done.7) | copy-start | bytes 393220
  80.8 13.5 %copy-start.11 = (f32[4,64,128]{2,1,0:T(8,128)S(1)}, f32[4,64,128]{2,1,0:T(8,128)}, u32[]{:S(2)}) copy-start(f32[4,64,128]{2,1,0:T(8,128)} %copy-done.10) | copy-start | bytes 393220
  80.9 13.5 %copy-start.14 = (f32[4,64,128]{2,1,0:T(8,128)S(1)}, f32[4,64,128]{2,1,0:T(8,128)}, u32[]{:S(2)}) copy-start(f32[4,64,128]{2,1,0:T(8,128)} %copy-done.13) | copy-start | bytes 393220
  80.9 13.5 %copy-start.17 = (f32[4,64,128]{2,1,0:T(8,128)S(1)}, f32[4,64,128]{2,1,0:T(8,128)}, u32[]{:S(2)}) copy-start(f32[4,64,128]{2,1,0:T(8,128)} %copy-done.16) | copy-start | bytes 393220
  80.9 13.5 %copy-start.20 = (f32[4,64,128]{2,1,0:T(8,128)S(1)}, f32[4,64,128]{2,1,0:T(8,128)}, u32[]{:S(2)}) copy-start(f32[4,64,128]{2,1,0:T(8,128)} %copy-done.19) | copy-start | bytes 393220
  80.9 13.5 %copy-start.23 = (f32[4,64,128]{2,1,0:T(8,128)S(1)}, f32[4,64,128]{2,1,0:T(8,128)}, u32[]{:S(2)}) copy-start(f32[4,64,128]{2,1,0:T(8,128)} %copy-done.22) | copy-start | bytes 393220
  80.9 13.5 %copy-start.34 = (f32[4,64,128]{2,1,0:T(8,128)S(1)}, f32[4,64,128]{2,1,0:T(8,128)}, u32[]{:S(2)}) copy-start(f32[4,64,128]{2,1,0:T(8,128)} %copy-done.33) | copy-start | bytes 393220
  80.9 13.5 %copy-start.37 = (f32[4,64,128]{2,1,0:T(8,128)S(1)}, f32[4,64,128]{2,1,0:T(8,128)}, u32[]{:S(2)}) copy-start(f32[4,64,128]{2,1,0:T(8,128)} %copy-done.36) | copy-start | bytes 393220
  80.9 13.5 %copy-start.40 = (f32[4,64,128]{2,1,0:T(8,128)S(1)}, f32[4,64,128]{2,1,0:T(8,128)}, u32[]{:S(2)}) copy-start(f32[4,64,128]{2,1,0:T(8,128)} %copy-done.39) | copy-start | bytes 393220
  100.6 37.6 %collective-permute-start.7 = (f32[9,1,64,128]{3,2,1,0:T(8,128)}, f32[9,1,64,128]{3,2,1,0:T(8,128)}, u32[]{:S(2)}, u32[]{:S(2)}) collective-permute-start(f32[9,1,64,128]{3,2,1,0:T(8,128)} %get-tuple-element.22), channel_id=1, source_target_pairs={{0,2},{2,4},{4,6},{6,8},{8,10},{10,12},{12,14},{14,16},{16,18},{18... | collective-permute-start | bytes 884744 | tf_op jit(solution)/shard_map/ppermute | solution.py:15
  105.0 33.3 %collective-permute-start.6 = (f32[9,1,64,128]{3,2,1,0:T(8,128)}, f32[9,1,64,128]{3,2,1,0:T(8,128)}, u32[]{:S(2)}, u32[]{:S(2)}) collective-permute-start(f32[9,1,64,128]{3,2,1,0:T(8,128)} %get-tuple-element.23), channel_id=1, source_target_pairs={{2,0},{4,2},{6,4},{8,6},{10,8},{12,10},{14,12},{16,14},{18,16},{20... | collective-permute-start | bytes 884744 | tf_op jit(solution)/shard_map/ppermute | solution.py:18
  138.1 4.1 %copy-start.18 = (f32[4,64,128]{2,1,0:T(8,128)S(1)}, f32[4,64,128]{2,1,0:T(8,128)}, u32[]{:S(2)}) copy-start(f32[4,64,128]{2,1,0:T(8,128)} %copy-done.16) | copy-start | bytes 393220
  138.1 4.1 %copy-start.21 = (f32[4,64,128]{2,1,0:T(8,128)S(1)}, f32[4,64,128]{2,1,0:T(8,128)}, u32[]{:S(2)}) copy-start(f32[4,64,128]{2,1,0:T(8,128)} %copy-done.19) | copy-start | bytes 393220
  138.1 4.1 %copy-start.24 = (f32[4,64,128]{2,1,0:T(8,128)S(1)}, f32[4,64,128]{2,1,0:T(8,128)}, u32[]{:S(2)}) copy-start(f32[4,64,128]{2,1,0:T(8,128)} %copy-done.22) | copy-start | bytes 393220
  138.2 4.1 %copy-start.26 = (f32[4,64,128]{2,1,0:T(8,128)S(1)}, f32[4,64,128]{2,1,0:T(8,128)}, u32[]{:S(2)}) copy-start(f32[4,64,128]{2,1,0:T(8,128)} %copy-done.25) | copy-start | bytes 393220
  138.2 4.1 %copy-start.28 = (f32[4,64,128]{2,1,0:T(8,128)S(1)}, f32[4,64,128]{2,1,0:T(8,128)}, u32[]{:S(2)}) copy-start(f32[4,64,128]{2,1,0:T(8,128)} %copy-done.27) | copy-start | bytes 393220
  138.2 4.1 %copy-start.30 = (f32[4,64,128]{2,1,0:T(8,128)S(1)}, f32[4,64,128]{2,1,0:T(8,128)}, u32[]{:S(2)}) copy-start(f32[4,64,128]{2,1,0:T(8,128)} %copy-done.29) | copy-start | bytes 393220
  138.2 4.1 %copy-start.32 = (f32[4,64,128]{2,1,0:T(8,128)S(1)}, f32[4,64,128]{2,1,0:T(8,128)}, u32[]{:S(2)}) copy-start(f32[4,64,128]{2,1,0:T(8,128)} %copy-done.31) | copy-start | bytes 393220
  138.2 4.1 %copy-start.35 = (f32[4,64,128]{2,1,0:T(8,128)S(1)}, f32[4,64,128]{2,1,0:T(8,128)}, u32[]{:S(2)}) copy-start(f32[4,64,128]{2,1,0:T(8,128)} %copy-done.33) | copy-start | bytes 393220
  138.2 4.1 %copy-start.38 = (f32[4,64,128]{2,1,0:T(8,128)S(1)}, f32[4,64,128]{2,1,0:T(8,128)}, u32[]{:S(2)}) copy-start(f32[4,64,128]{2,1,0:T(8,128)} %copy-done.36) | copy-start | bytes 393220
  138.2 4.1 %copy-start.41 = (f32[4,64,128]{2,1,0:T(8,128)S(1)}, f32[4,64,128]{2,1,0:T(8,128)}, u32[]{:S(2)}) copy-start(f32[4,64,128]{2,1,0:T(8,128)} %copy-done.39) | copy-start | bytes 393220
  138.2 4.1 %copy-start.43 = (f32[4,64,128]{2,1,0:T(8,128)S(1)}, f32[4,64,128]{2,1,0:T(8,128)}, u32[]{:S(2)}) copy-start(f32[4,64,128]{2,1,0:T(8,128)} %get-tuple-element.42) | copy-start | bytes 393220
  138.2 4.1 %copy-start.45 = (f32[4,64,128]{2,1,0:T(8,128)S(1)}, f32[4,64,128]{2,1,0:T(8,128)}, u32[]{:S(2)}) copy-start(f32[4,64,128]{2,1,0:T(8,128)} %get-tuple-element.65) | copy-start | bytes 393220
  148.6 8.8 %copy-start = (f32[8,4,64,128]{3,2,1,0:T(8,128)}, f32[8,4,64,128]{3,2,1,0:T(8,128)S(1)}, u32[]{:S(2)}) copy-start(f32[8,4,64,128]{3,2,1,0:T(8,128)S(1)} %fusion.84) | copy-start | bytes 3145732
  148.6 15.2 %copy-start.51 = (f32[128,8]{1,0:T(8,128)S(1)}, f32[128,8]{1,0:T(8,128)}, u32[]{:S(2)}) copy-start(f32[128,8]{1,0:T(8,128)} %gather_fusion) | copy-start | bytes 12292
  148.6 15.2 %copy-start.52 = (f32[128,8]{1,0:T(8,128)S(1)}, f32[128,8]{1,0:T(8,128)}, u32[]{:S(2)}) copy-start(f32[128,8]{1,0:T(8,128)} %gather_fusion.1) | copy-start | bytes 12292
  148.6 15.2 %copy-start.54 = (pred[128]{0:T(512)(128)(4,1)S(1)}, pred[128]{0:T(512)(128)(4,1)}, u32[]{:S(2)}) copy-start(pred[128]{0:T(512)(128)(4,1)} %get-tuple-element.8) | copy-start | bytes 388
  148.6 15.2 %copy-start.55 = (pred[128]{0:T(512)(128)(4,1)S(1)}, pred[128]{0:T(512)(128)(4,1)}, u32[]{:S(2)}) copy-start(pred[128]{0:T(512)(128)(4,1)} %get-tuple-element.56) | copy-start | bytes 388
  148.6 15.2 %copy-start.56 = (pred[128]{0:T(512)(128)(4,1)S(1)}, pred[128]{0:T(512)(128)(4,1)}, u32[]{:S(2)}) copy-start(pred[128]{0:T(512)(128)(4,1)} %get-tuple-element.55) | copy-start | bytes 388
  (6 other events, 21.4 us)
Sparse Core Ops, SparseCore 0:
  25.5 20.9 all-reduce.6
where the time goes:
time: 250 us; the launch traced here: 249 us
  blocking collectives  80.2 us (32%)
  local copies, waits for them, and re-layouts  49.8 us (20%)
  waiting for transfers between devices  41.6 us (17%)
  other arithmetic  32.7 us (13%)
  between operations  23 us (9%)
  starting transfers between devices  21.6 us (9%)
    psum x1, blocking collectives, body(): release_grad = lax.psum(partial_grad, 'space')  77.5 us
    add x3, local copies, waits for them, and re-layouts, body(): lam = mixed + applied[1:] + retard_slope(conc) * applied[0] * mixed  26 us
    ppermute x4, waiting for transfers between devices, extended(): lax.ppermute(lax.slice_in_dim(block, block.shape[dim] - width, None, axis...  21.2 us
    gather x3, local copies, waits for them, and re-layouts, body(): values = jnp.take(lam.reshape(own_sensors, cells), release_index, axis=1)  20.4 us
    psum x1, waiting for transfers between devices, broadcast(): return lax.psum(jnp.where(mine, array, jnp.zeros_like(array)), axis)  17.7 us
    ppermute x4, starting transfers between devices, extended(): lax.ppermute(lax.slice_in_dim(block, block.shape[dim] - width, None, axis...  16.2 us
    add x3, other arithmetic, apply_op(): total = total + 0.5 * sign * flux  15 us
    concatenate x4, other arithmetic, extended(): block = jnp.concatenate([low, block, high], axis=dim)  9.99 us
  transfers between devices with their start and end apart: 9, of which 5 were waited for; matrix products, arithmetic and copies ran while one was open for 15% of the time, Pallas kernels for 0%

commit v1 on v0

--- a/solution.py
+++ b/solution.py
@@ -5,6 +5,15 @@
 
 STEPS = 3
 step_dt = 0.12
+
+
+def sum_by_hops(array, name):
+    size = lax.axis_size(name)
+    result, hop = (array, 1)
+    while hop < size:
+        result = result + lax.ppermute(result, name, [(i, i ^ hop) for i in range(size)])
+        hop = 2 * hop
+    return result
 
 
 def extended(block, sides, width):
@@ -121,7 +130,7 @@
         values = jnp.take(lam.reshape(own_sensors, cells), release_index, axis=1)
         keep = release_inside & (release_steps == step)
         partial_grad = partial_grad + jnp.where(keep[None, :], values, 0.0)
-    release_grad = lax.psum(partial_grad, "space")
+    release_grad = sum_by_hops(partial_grad, "space")
     return (lam, release_grad)
 
 

time: 250 us -> 195 us (0.78)
  blocking collectives: 80.2 us -> 2.79 us
  starting transfers between devices: 21.6 us -> 32.9 us
  waiting for transfers between devices: 41.6 us -> 52.5 us
    psum x1 -> x0, blocking collectives: 77.5 us -> none  [body(): release_grad = lax.psum(partial_grad, 'space')]
    ppermute x0 -> x4, starting transfers between devices: none -> 11.3 us  [sum_by_hops(): lax.ppermute(result, name, [(i, i ^ hop) for i in range(size)])]
    ppermute x0 -> x4, waiting for transfers between devices: none -> 10.7 us  [sum_by_hops(): lax.ppermute(result, name, [(i, i ^ hop) for i in range(size)])]
  transfers between devices with their start and end apart: 9 -> 13, of which waited for: 5 -> 9; matrix products, arithmetic and copies ran while one was open for 15% -> 19% of each run, Pallas kernels for 0% -> 0%
where the time goes in v1:
time: 195 us; the launch traced here: 194 us
  waiting for transfers between devices  52.5 us (27%)
  local copies, waits for them, and re-layouts  50 us (26%)
  starting transfers between devices  32.9 us (17%)
  other arithmetic  32.7 us (17%)
  between operations  22.9 us (12%)
  blocking collectives  2.79 us (1%)
    add x3, local copies, waits for them, and re-layouts, body(): lam = mixed + applied[1:] + retard_slope(conc) * applied[0] * mixed  26.2 us
    ppermute x4, waiting for transfers between devices, extended(): lax.ppermute(lax.slice_in_dim(block, block.shape[dim] - width, None, axis...  21.3 us
    gather x3, local copies, waits for them, and re-layouts, body(): values = jnp.take(lam.reshape(own_sensors, cells), release_index, axis=1)  20.4 us
    psum x1, waiting for transfers between devices, broadcast(): return lax.psum(jnp.where(mine, array, jnp.zeros_like(array)), axis)  17.7 us
    ppermute x4, starting transfers between devices, extended(): lax.ppermute(lax.slice_in_dim(block, block.shape[dim] - width, None, axis...  16.2 us
    add x3, other arithmetic, apply_op(): total = total + 0.5 * sign * flux  15 us
    ppermute x4, starting transfers between devices, sum_by_hops(): lax.ppermute(result, name, [(i, i ^ hop) for i in range(size)])  11.3 us
    ppermute x4, waiting for transfers between devices, sum_by_hops(): lax.ppermute(result, name, [(i, i ^ hop) for i in range(size)])  10.7 us
  transfers between devices with their start and end apart: 13, of which 9 were waited for; matrix products, arithmetic and copies ran while one was open for 19% of the time, Pallas kernels for 0%

profile of v1, /device:TPU:0, one launch (start us, length us, event | category | flops | bytes accessed | tf_op | source)
XLA Modules:
  0.0 193.9 jit_solution(5476605386013216134)
XLA Ops:
  7.2 0.0 all-reduce.7.cloned.1.call-start
  7.2 2.8 %all_gather.3 = f32[6,4,64,128]{3,2,1,0:T(8,128)S(1)} all-gather(f32[6,4,32,128]{3,2,1,0:T(8,128)} %param.12), channel_id=1, replica_groups=mesh['space'=16,'sens'=2] {'sens'}, dimensions={2}, use_global_device_ids=true | all-gather | bytes 1179648 | tf_op jit(solution)/shard_map/all_gather | solution.py:116
  10.1 4.8 %collective-permute-start = (f32[6,1,64,128]{3,2,1,0:T(8,128)S(1)}, f32[6,1,64,128]{3,2,1,0:T(8,128)S(1)}, u32[]{:S(2)}, u32[]{:S(2)}) collective-permute-start(f32[6,1,64,128]{3,2,1,0:T(8,128)S(1)} %get-tuple-element.28), channel_id=1, source_target_pairs={{0,2},{2,4},{4,6},{6,8},{8,10},{10,12},{12,14},{14,16},{16,18},{18... | collective-permute-start | bytes 589832 | tf_op jit(solution)/shard_map/ppermute | solution.py:24
  14.8 1.3 collective-permute-start.1
  16.2 0.6 fusion.113
  24.5 0.8 select_bitcast_fusion
  25.3 0.0 all-reduce.7.cloned.1.call-update
  25.4 0.8 select_maximum_fusion.9
  26.2 1.2 slice_bitcast_fusion.5
  27.4 1.0 slice_multiply_fusion.11
  28.4 0.3 slice_multiply_fusion.3
  28.7 17.7 %all-reduce.7.cloned.1.call-done = (f32[4,64,128]{2,1,0:T(8,128)}, f32[4,64,128]{2,1,0:T(8,128)}, f32[4,64,128]{2,1,0:T(8,128)}) async-done(((f32[4,64,128]{2,1,0:T(8,128)}, f32[4,64,128]{2,1,0:T(8,128)}, f32[4,64,128]{2,1,0:T(8,128)}), (f32[4,64,128]{2,1,0:T(8,128)}, f32[4,64,128]{2,1,0:T(8,128)}, f32[4,64,128]{2,1,0:T(8,128)})) %all-reduce.7.cloned.1.call-update) | async-done | bytes 393232 | tf_op jit(solution)/shard_map/psum | solution.py:34
  46.5 1.0 fusion.107
  47.5 0.3 fusion.89
  47.7 0.0 copy-start.48
  47.8 0.6 copy-done.4
  48.4 3.7 %collective-permute-start.3 = (f32[9,1,64,128]{3,2,1,0:T(8,128)S(1)}, f32[9,1,64,128]{3,2,1,0:T(8,128)S(1)}, u32[]{:S(2)}, u32[]{:S(2)}) collective-permute-start(f32[9,1,64,128]{3,2,1,0:T(8,128)S(1)} %get-tuple-element.26), channel_id=1, source_target_pairs={{0,2},{2,4},{4,6},{6,8},{8,10},{10,12},{12,14},{14,16},{16,18},{18... | collective-permute-start | bytes 884744 | tf_op jit(solution)/shard_map/ppermute | solution.py:24
  52.1 1.3 collective-permute-start.2
  53.4 0.3 fusion.102
  53.8 0.1 fusion.106
  53.9 11.3 %collective-permute-done.3 = f32[9,1,64,128]{3,2,1,0:T(8,128)S(1)} collective-permute-done((f32[9,1,64,128]{3,2,1,0:T(8,128)S(1)}, f32[9,1,64,128]{3,2,1,0:T(8,128)S(1)}, u32[]{:S(2)}, u32[]{:S(2)}) %collective-permute-start.3) | collective-permute-done | bytes 294944 | tf_op jit(solution)/shard_map/ppermute | solution.py:24
  65.1 1.9 collective-permute-done.2
  67.0 2.7 %select_maximum_fusion.6 = f32[9,6,66,130]{3,2,1,0:T(8,128)S(1)} fusion(f32[9,1,64,128]{3,2,1,0:T(8,128)S(1)} %collective-permute-done.2, f32[9,1,64,128]{3,2,1,0:T(8,128)S(1)} %collective-permute-done.3, f32[8,4,64,128]{3,2,1,0:T(8,128)S(1)} %fusion.89, f32[1,4,64,128]{3,2,1,0:T(8,128)S(1)} %bitcast.69), kind=kLoop, calls=%fused_computation.13 | loop fusion | flops 8339760 | bytes 3622752 | tf_op jit(solution)/shard_map/concatenate | solution.py:28
  69.8 4.7 %fusion.69 = f32[9,4,64,128]{3,2,1,0:T(8,128)S(1)} fusion(f32[9,6,66,130]{3,2,1,0:T(8,128)S(1)} %select_maximum_fusion.6, f32[9,1,64,128]{3,2,1,0:T(8,128)S(1)} %collective-permute-done.3, f32[8,4,64,128]{3,2,1,0:T(8,128)S(1)} %fusion.89, f32[1,4,64,128]{3,2,1,0:T(8,128)S(1)} %bitcast.70, f32[9,1,64,128]{3,2,1,0:T(8,128)S(1)} %collective-permute-done.2, ...), kind=kLoop, calls=%fused_computation.120 | loop fusion | flops 20643840 | bytes 24182784 | tf_op jit(solution)/shard_map/add | solution.py:84
  74.5 0.1 fusion.98
  74.6 0.6 fusion.88
  75.2 0.0 copy-start.57
  75.2 0.0 copy-start.59
  75.3 3.4 %collective-permute-start.5 = (f32[9,1,64,128]{3,2,1,0:T(8,128)S(1)}, f32[9,1,64,128]{3,2,1,0:T(8,128)S(1)}, u32[]{:S(2)}, u32[]{:S(2)}) collective-permute-start(f32[9,1,64,128]{3,2,1,0:T(8,128)S(1)} %get-tuple-element.24), channel_id=1, source_target_pairs={{0,2},{2,4},{4,6},{6,8},{8,10},{10,12},{12,14},{14,16},{16,18},{18... | collective-permute-start | bytes 884744 | tf_op jit(solution)/shard_map/ppermute | solution.py:24
  78.7 1.5 collective-permute-start.4
  80.2 0.5 compare_and_fusion.3
  80.7 0.1 fusion.105
  80.9 10.0 %collective-permute-done.5 = f32[9,1,64,128]{3,2,1,0:T(8,128)S(1)} collective-permute-done((f32[9,1,64,128]{3,2,1,0:T(8,128)S(1)}, f32[9,1,64,128]{3,2,1,0:T(8,128)S(1)}, u32[]{:S(2)}, u32[]{:S(2)}) %collective-permute-start.5) | collective-permute-done | bytes 294944 | tf_op jit(solution)/shard_map/ppermute | solution.py:24
  90.9 0.7 collective-permute-done.4
  91.6 2.7 %select_maximum_fusion.3 = f32[9,6,66,130]{3,2,1,0:T(8,128)S(1)} fusion(f32[9,1,64,128]{3,2,1,0:T(8,128)S(1)} %collective-permute-done.4, f32[9,1,64,128]{3,2,1,0:T(8,128)S(1)} %collective-permute-done.5, f32[8,4,64,128]{3,2,1,0:T(8,128)S(1)} %get-tuple-element.14, f32[1,4,64,128]{3,2,1,0:T(8,128)S(1)} %bitcast.66), kind=kLoop, calls=%fused_computation.10 | loop fusion | flops 8339760 | bytes 3622752 | tf_op jit(solution)/shard_map/concatenate | solution.py:28
  94.4 4.7 %fusion.44 = f32[9,4,64,128]{3,2,1,0:T(8,128)S(1)} fusion(f32[9,6,66,130]{3,2,1,0:T(8,128)S(1)} %select_maximum_fusion.3, f32[9,1,64,128]{3,2,1,0:T(8,128)S(1)} %collective-permute-done.5, f32[8,4,64,128]{3,2,1,0:T(8,128)S(1)} %get-tuple-element.14, f32[1,4,64,128]{3,2,1,0:T(8,128)S(1)} %bitcast.67, f32[9,1,64,128]{3,2,1,0:T(8,128)S(1)} %collective-permute-done.4, ...), kind=kLoop, calls=%fused_computation.87 | loop fusion | flops 20643840 | bytes 24182784 | tf_op jit(solution)/shard_map/add | solution.py:84
  99.1 0.1 fusion.97
  99.2 0.6 fusion.87
  99.8 0.9 fusion.91
  100.7 4.4 %collective-permute-start.7 = (f32[9,1,64,128]{3,2,1,0:T(8,128)}, f32[9,1,64,128]{3,2,1,0:T(8,128)}, u32[]{:S(2)}, u32[]{:S(2)}) collective-permute-start(f32[9,1,64,128]{3,2,1,0:T(8,128)} %get-tuple-element.22), channel_id=1, source_target_pairs={{0,2},{2,4},{4,6},{6,8},{8,10},{10,12},{12,14},{14,16},{16,18},{18... | collective-permute-start | bytes 884744 | tf_op jit(solution)/shard_map/ppermute | solution.py:24
  105.0 1.3 collective-permute-start.6
  106.3 0.5 compare_and_fusion.2
  106.8 8.7 %copy.10 = f32[8,4,64,128]{0,3,2,1:T(8,128)} copy(f32[8,4,64,128]{3,2,1,0:T(8,128)S(1)} %get-tuple-element.15) | data formatting | bytes 2097152 | tf_op jit(solution)/shard_map/add | solution.py:129
  115.6 7.0 %gather_fusion = f32[128,8]{1,0:T(8,128)} fusion(f32[8,32768]{0,1:T(8,128)} %bitcast.59, s32[1024]{0:T(1024)S(1)} %pad_clamp_fusion), kind=kCustom, calls=%fused_computation.clone | custom fusion | bytes 8704 | tf_op jit(solution)/shard_map/jit(_take)/gather | solution.py:130
  122.6 8.7 %copy.11 = f32[8,4,64,128]{0,3,2,1:T(8,128)} copy(f32[8,4,64,128]{3,2,1,0:T(8,128)S(1)} %get-tuple-element.13) | data formatting | bytes 2097152 | tf_op jit(solution)/shard_map/add | solution.py:129
  131.3 7.0 %gather_fusion.1 = f32[128,8]{1,0:T(8,128)} fusion(f32[8,32768]{0,1:T(8,128)} %bitcast.61, s32[1024]{0:T(1024)S(1)} %pad_clamp_fusion), kind=kCustom, calls=%fused_computation.1.clone | custom fusion | bytes 8704 | tf_op jit(solution)/shard_map/jit(_take)/gather | solution.py:130
  138.5 3.9 %select_maximum_fusion = f32[9,6,66,130]{3,2,1,0:T(8,128)S(1)} fusion(f32[9,1,64,128]{3,2,1,0:T(8,128)} %collective-permute-done.6, f32[9,1,64,128]{3,2,1,0:T(8,128)} %collective-permute-done.7, f32[8,4,64,128]{3,2,1,0:T(8,128)S(1)} %get-tuple-element.12, f32[1,4,64,128]{3,2,1,0:T(8,128)S(1)} %bitcast.63), kind=kLoop, calls=%fused_computation.7 | loop fusion | flops 8339760 | bytes 3622752 | tf_op jit(solution)/shard_map/concatenate | solution.py:28
  142.6 5.7 %fusion.19 = f32[9,4,64,128]{3,2,1,0:T(8,128)S(1)} fusion(f32[9,6,66,130]{3,2,1,0:T(8,128)S(1)} %select_maximum_fusion, f32[9,1,64,128]{3,2,1,0:T(8,128)} %collective-permute-done.7, f32[8,4,64,128]{3,2,1,0:T(8,128)S(1)} %get-tuple-element.12, f32[1,4,64,128]{3,2,1,0:T(8,128)S(1)} %bitcast.64, f32[9,1,64,128]{3,2,1,0:T(8,128)} %collective-permute-done.6, ...), kind=kLoop, calls=%fused_computation.54 | loop fusion | flops 20643840 | bytes 24182784 | tf_op jit(solution)/shard_map/add | solution.py:84
  148.3 0.1 fusion.96
  148.4 0.4 fusion.84
  148.8 0.0 copy-start
  148.8 0.0 copy-start.54
  148.9 8.8 %copy.12 = f32[8,4,64,128]{0,3,2,1:T(8,128)} copy(f32[8,4,64,128]{3,2,1,0:T(8,128)S(1)} %fusion.84) | data formatting | bytes 2097152 | tf_op jit(solution)/shard_map/add | solution.py:129
  157.6 6.4 %gather_fusion.2 = f32[128,8]{1,0:T(8,128)S(1)} fusion(f32[8,32768]{0,1:T(8,128)} %bitcast.60, s32[1024]{0:T(1024)S(1)} %pad_clamp_fusion), kind=kCustom, calls=%fused_computation.2.clone | custom fusion | bytes 8704 | tf_op jit(solution)/shard_map/jit(_take)/gather | solution.py:130
  164.1 0.1 fusion.108
  164.2 2.7 %collective-permute-start.8 = (f32[8,128]{0,1:T(8,128)S(1)}, f32[8,128]{0,1:T(8,128)S(1)}, u32[]{:S(2)}, u32[]{:S(2)}) collective-permute-start(f32[8,128]{0,1:T(8,128)S(1)} %fusion.108), channel_id=1, source_target_pairs={{0,2},{2,0},{4,6},{6,4},{8,10},{10,8},{12,14},{14,12},{16,18},{18,... | collective-permute-start | bytes 12296 | tf_op jit(solution)/shard_map/ppermute | solution.py:14
  167.0 2.2 %collective-permute-done.8 = f32[8,128]{0,1:T(8,128)S(1)} collective-permute-done((f32[8,128]{0,1:T(8,128)S(1)}, f32[8,128]{0,1:T(8,128)S(1)}, u32[]{:S(2)}, u32[]{:S(2)}) %collective-permute-start.8) | collective-permute-done | bytes 4128 | tf_op jit(solution)/shard_map/ppermute | solution.py:14
  169.2 1.7 collective-permute-start.9
  170.9 2.6 %collective-permute-done.9 = f32[8,128]{0,1:T(8,128)S(1)} collective-permute-done((f32[8,128]{0,1:T(8,128)S(1)}, f32[8,128]{0,1:T(8,128)S(1)}, u32[]{:S(2)}, u32[]{:S(2)}) %collective-permute-start.9) | collective-permute-done | bytes 4128 | tf_op jit(solution)/shard_map/ppermute | solution.py:14
  173.6 4.6 %collective-permute-start.10 = (f32[8,128]{0,1:T(8,128)S(1)}, f32[8,128]{0,1:T(8,128)S(1)}, u32[]{:S(2)}, u32[]{:S(2)}) collective-permute-start(f32[8,128]{0,1:T(8,128)S(1)} %add.337), channel_id=1, source_target_pairs={{0,8},{2,10},{4,12},{6,14},{8,0},{10,2},{12,4},{14,6},{16,24},{18,... | collective-permute-start | bytes 12296 | tf_op jit(solution)/shard_map/ppermute | solution.py:14
  178.2 2.9 %collective-permute-done.10 = f32[8,128]{0,1:T(8,128)S(1)} collective-permute-done((f32[8,128]{0,1:T(8,128)S(1)}, f32[8,128]{0,1:T(8,128)S(1)}, u32[]{:S(2)}, u32[]{:S(2)}) %collective-permute-start.10) | collective-permute-done | bytes 4128 | tf_op jit(solution)/shard_map/ppermute | solution.py:14
  181.1 2.3 %collective-permute-start.11 = (f32[8,128]{0,1:T(8,128)S(1)}, f32[8,128]{0,1:T(8,128)S(1)}, u32[]{:S(2)}, u32[]{:S(2)}) collective-permute-start(f32[8,128]{0,1:T(8,128)S(1)} %add.338), channel_id=1, source_target_pairs={{0,16},{2,18},{4,20},{6,22},{8,24},{10,26},{12,28},{14,30},{16,0},... | collective-permute-start | bytes 12296 | tf_op jit(solution)/shard_map/ppermute | solution.py:14
  183.4 2.9 %collective-permute-done.11 = f32[8,128]{0,1:T(8,128)S(1)} collective-permute-done((f32[8,128]{0,1:T(8,128)S(1)}, f32[8,128]{0,1:T(8,128)S(1)}, u32[]{:S(2)}, u32[]{:S(2)}) %collective-permute-start.11) | collective-permute-done | bytes 4128 | tf_op jit(solution)/shard_map/ppermute | solution.py:14
  186.4 0.7 copy.13
  (131 shorter events, 0.4 us)
Async XLA Ops:
  7.2 9.0 %copy-start.53 = (s32[3]{0:T(128)S(1)}, s32[3]{0:T(128)}, u32[]{:S(2)}) copy-start(s32[3]{0:T(128)} %param.13) | copy-start | bytes 40
  7.2 17.4 %copy-start.50 = (f32[4,4,64,128]{3,2,1,0:T(8,128)S(1)}, f32[4,4,64,128]{3,2,1,0:T(8,128)}, u32[]{:S(2)}) copy-start(f32[4,4,64,128]{3,2,1,0:T(8,128)} %param.11) | copy-start | bytes 1572868
  7.2 39.3 %all-reduce.7.cloned.1.call-start = ((), (), s32[]{:S(2)}) async-start(), calls=%async_computation | async-start | bytes 786432 | tf_op jit(solution)/shard_map/psum | solution.py:34
  10.0 15.4 %copy-start.58 = (f32[8,3]{0,1:T(4,128)S(1)}, f32[8,3]{0,1:T(4,128)}, u32[]{:S(2)}) copy-start(f32[8,3]{0,1:T(4,128)} %param.15) | copy-start | bytes 292
  10.0 15.4 %copy-start.60 = (s32[8]{0:T(128)S(1)}, s32[8]{0:T(128)}, u32[]{:S(2)}) copy-start(s32[8]{0:T(128)} %param.14) | copy-start | bytes 100
  10.1 15.4 %collective-permute-start = (f32[6,1,64,128]{3,2,1,0:T(8,128)S(1)}, f32[6,1,64,128]{3,2,1,0:T(8,128)S(1)}, u32[]{:S(2)}, u32[]{:S(2)}) collective-permute-start(f32[6,1,64,128]{3,2,1,0:T(8,128)S(1)} %get-tuple-element.28), channel_id=1, source_target_pairs={{0,2},{2,4},{4,6},{6,8},{8,10},{10,12},{12,14},{14,16},{16,18},{18... | collective-permute-start | bytes 589832 | tf_op jit(solution)/shard_map/ppermute | solution.py:24
  14.8 10.6 %collective-permute-start.1 = (f32[6,1,64,128]{3,2,1,0:T(8,128)S(1)}, f32[6,1,64,128]{3,2,1,0:T(8,128)S(1)}, u32[]{:S(2)}, u32[]{:S(2)}) collective-permute-start(f32[6,1,64,128]{3,2,1,0:T(8,128)S(1)} %get-tuple-element.29), channel_id=1, source_target_pairs={{2,0},{4,2},{6,4},{8,6},{10,8},{12,10},{14,12},{16,14},{18,16},{20... | collective-permute-start | bytes 589832 | tf_op jit(solution)/shard_map/ppermute | solution.py:27
  28.4 41.3 %copy-start.33 = (f32[4,64,128]{2,1,0:T(8,128)}, f32[4,64,128]{2,1,0:T(8,128)S(1)}, u32[]{:S(2)}) copy-start(f32[4,64,128]{2,1,0:T(8,128)S(1)} %get-tuple-element.39) | copy-start | bytes 393220
  28.4 41.4 %copy-start.36 = (f32[4,64,128]{2,1,0:T(8,128)}, f32[4,64,128]{2,1,0:T(8,128)S(1)}, u32[]{:S(2)}) copy-start(f32[4,64,128]{2,1,0:T(8,128)S(1)} %get-tuple-element.40) | copy-start | bytes 393220
  28.4 41.4 %copy-start.39 = (f32[4,64,128]{2,1,0:T(8,128)}, f32[4,64,128]{2,1,0:T(8,128)S(1)}, u32[]{:S(2)}) copy-start(f32[4,64,128]{2,1,0:T(8,128)S(1)} %get-tuple-element.41) | copy-start | bytes 393220
  28.4 19.1 %copy-start.1 = (f32[8,4,64,128]{3,2,1,0:T(8,128)S(1)}, f32[8,4,64,128]{3,2,1,0:T(8,128)}, u32[]{:S(2)}) copy-start(f32[8,4,64,128]{3,2,1,0:T(8,128)} %param.10) | copy-start | bytes 3145732
  28.7 41.1 %copy-start.7 = (f32[4,64,128]{2,1,0:T(8,128)}, f32[4,64,128]{2,1,0:T(8,128)S(1)}, u32[]{:S(2)}) copy-start(f32[4,64,128]{2,1,0:T(8,128)S(1)} %get-tuple-element.49) | copy-start | bytes 393220
  28.7 41.1 %copy-start.10 = (f32[4,64,128]{2,1,0:T(8,128)}, f32[4,64,128]{2,1,0:T(8,128)S(1)}, u32[]{:S(2)}) copy-start(f32[4,64,128]{2,1,0:T(8,128)S(1)} %get-tuple-element.50) | copy-start | bytes 393220
  28.7 41.1 %copy-start.13 = (f32[4,64,128]{2,1,0:T(8,128)}, f32[4,64,128]{2,1,0:T(8,128)S(1)}, u32[]{:S(2)}) copy-start(f32[4,64,128]{2,1,0:T(8,128)S(1)} %get-tuple-element.61) | copy-start | bytes 393220
  28.7 41.1 %copy-start.16 = (f32[4,64,128]{2,1,0:T(8,128)}, f32[4,64,128]{2,1,0:T(8,128)S(1)}, u32[]{:S(2)}) copy-start(f32[4,64,128]{2,1,0:T(8,128)S(1)} %get-tuple-element.62) | copy-start | bytes 393220
  28.7 41.1 %copy-start.19 = (f32[4,64,128]{2,1,0:T(8,128)}, f32[4,64,128]{2,1,0:T(8,128)S(1)}, u32[]{:S(2)}) copy-start(f32[4,64,128]{2,1,0:T(8,128)S(1)} %get-tuple-element.63) | copy-start | bytes 393220
  28.7 41.1 %copy-start.22 = (f32[4,64,128]{2,1,0:T(8,128)}, f32[4,64,128]{2,1,0:T(8,128)S(1)}, u32[]{:S(2)}) copy-start(f32[4,64,128]{2,1,0:T(8,128)S(1)} %get-tuple-element.64) | copy-start | bytes 393220
  28.7 65.6 %copy-start.5 = (f32[4,64,128]{2,1,0:T(8,128)}, f32[4,64,128]{2,1,0:T(8,128)S(1)}, u32[]{:S(2)}) copy-start(f32[4,64,128]{2,1,0:T(8,128)S(1)} %get-tuple-element.48) | copy-start | bytes 393220
  47.7 5.7 %copy-start.48 = (f32[6,66,130]{2,1,0:T(8,128)S(1)}, f32[6,66,130]{2,1,0:T(8,128)}, u32[]{:S(2)}) copy-start(f32[6,66,130]{2,1,0:T(8,128)} %get-tuple-element.16) | copy-start | bytes 617764
  47.8 5.7 %copy-start.49 = (f32[6,66,130]{2,1,0:T(8,128)S(1)}, f32[6,66,130]{2,1,0:T(8,128)}, u32[]{:S(2)}) copy-start(f32[6,66,130]{2,1,0:T(8,128)} %get-tuple-element.20) | copy-start | bytes 617764
  48.4 5.4 %copy-start.3 = (f32[4,64,128]{2,1,0:T(8,128)S(1)}, f32[4,64,128]{2,1,0:T(8,128)}, u32[]{:S(2)}) copy-start(f32[4,64,128]{2,1,0:T(8,128)} %get-tuple-element.6) | copy-start | bytes 393220
  48.4 16.7 %collective-permute-start.3 = (f32[9,1,64,128]{3,2,1,0:T(8,128)S(1)}, f32[9,1,64,128]{3,2,1,0:T(8,128)S(1)}, u32[]{:S(2)}, u32[]{:S(2)}) collective-permute-start(f32[9,1,64,128]{3,2,1,0:T(8,128)S(1)} %get-tuple-element.26), channel_id=1, source_target_pairs={{0,2},{2,4},{4,6},{6,8},{8,10},{10,12},{12,14},{14,16},{16,18},{18... | collective-permute-start | bytes 884744 | tf_op jit(solution)/shard_map/ppermute | solution.py:24
  52.1 14.9 %collective-permute-start.2 = (f32[9,1,64,128]{3,2,1,0:T(8,128)S(1)}, f32[9,1,64,128]{3,2,1,0:T(8,128)S(1)}, u32[]{:S(2)}, u32[]{:S(2)}) collective-permute-start(f32[9,1,64,128]{3,2,1,0:T(8,128)S(1)} %get-tuple-element.27), channel_id=1, source_target_pairs={{2,0},{4,2},{6,4},{8,6},{10,8},{12,10},{14,12},{16,14},{18,16},{20... | collective-permute-start | bytes 884744 | tf_op jit(solution)/shard_map/ppermute | solution.py:27
  53.7 40.6 %copy-start.25 = (f32[4,64,128]{2,1,0:T(8,128)}, f32[4,64,128]{2,1,0:T(8,128)S(1)}, u32[]{:S(2)}) copy-start(f32[4,64,128]{2,1,0:T(8,128)S(1)} %get-tuple-element.35) | copy-start | bytes 393220
  53.7 40.6 %copy-start.27 = (f32[4,64,128]{2,1,0:T(8,128)}, f32[4,64,128]{2,1,0:T(8,128)S(1)}, u32[]{:S(2)}) copy-start(f32[4,64,128]{2,1,0:T(8,128)S(1)} %get-tuple-element.36) | copy-start | bytes 393220
  53.7 40.6 %copy-start.29 = (f32[4,64,128]{2,1,0:T(8,128)}, f32[4,64,128]{2,1,0:T(8,128)S(1)}, u32[]{:S(2)}) copy-start(f32[4,64,128]{2,1,0:T(8,128)S(1)} %get-tuple-element.67) | copy-start | bytes 393220
  53.7 40.6 %copy-start.31 = (f32[4,64,128]{2,1,0:T(8,128)}, f32[4,64,128]{2,1,0:T(8,128)S(1)}, u32[]{:S(2)}) copy-start(f32[4,64,128]{2,1,0:T(8,128)S(1)} %get-tuple-element.68) | copy-start | bytes 393220
  53.8 16.0 %copy-start.42 = (f32[4,64,128]{2,1,0:T(8,128)S(1)}, f32[4,64,128]{2,1,0:T(8,128)}, u32[]{:S(2)}) copy-start(f32[4,64,128]{2,1,0:T(8,128)} %get-tuple-element.42) | copy-start | bytes 393220
  53.8 16.0 %copy-start.44 = (f32[4,64,128]{2,1,0:T(8,128)S(1)}, f32[4,64,128]{2,1,0:T(8,128)}, u32[]{:S(2)}) copy-start(f32[4,64,128]{2,1,0:T(8,128)} %get-tuple-element.65) | copy-start | bytes 393220
  53.9 16.0 %copy-start.46 = (f32[4,64,128]{2,1,0:T(8,128)S(1)}, f32[4,64,128]{2,1,0:T(8,128)}, u32[]{:S(2)}) copy-start(f32[4,64,128]{2,1,0:T(8,128)} %get-tuple-element.66) | copy-start | bytes 393220
  75.2 5.0 %copy-start.57 = (s32[128]{0:T(128)S(1)}, s32[128]{0:T(128)}, u32[]{:S(2)}) copy-start(s32[128]{0:T(128)} %param.17) | copy-start | bytes 1540
  75.2 5.0 %copy-start.59 = (s32[128]{0:T(128)S(1)}, s32[128]{0:T(128)}, u32[]{:S(2)}) copy-start(s32[128]{0:T(128)} %param.16) | copy-start | bytes 1540
  75.2 5.5 %copy-start.2 = (f32[4,64,128]{2,1,0:T(8,128)S(1)}, f32[4,64,128]{2,1,0:T(8,128)}, u32[]{:S(2)}) copy-start(f32[4,64,128]{2,1,0:T(8,128)} %get-tuple-element.7) | copy-start | bytes 393220
  75.3 15.6 %collective-permute-start.5 = (f32[9,1,64,128]{3,2,1,0:T(8,128)S(1)}, f32[9,1,64,128]{3,2,1,0:T(8,128)S(1)}, u32[]{:S(2)}, u32[]{:S(2)}) collective-permute-start(f32[9,1,64,128]{3,2,1,0:T(8,128)S(1)} %get-tuple-element.24), channel_id=1, source_target_pairs={{0,2},{2,4},{4,6},{6,8},{8,10},{10,12},{12,14},{14,16},{16,18},{18... | collective-permute-start | bytes 884744 | tf_op jit(solution)/shard_map/ppermute | solution.py:24
  78.7 12.9 %collective-permute-start.4 = (f32[9,1,64,128]{3,2,1,0:T(8,128)S(1)}, f32[9,1,64,128]{3,2,1,0:T(8,128)S(1)}, u32[]{:S(2)}, u32[]{:S(2)}) collective-permute-start(f32[9,1,64,128]{3,2,1,0:T(8,128)S(1)} %get-tuple-element.25), channel_id=1, source_target_pairs={{2,0},{4,2},{6,4},{8,6},{10,8},{12,10},{14,12},{16,14},{18,16},{20... | collective-permute-start | bytes 884744 | tf_op jit(solution)/shard_map/ppermute | solution.py:27
  80.8 13.6 %copy-start.8 = (f32[4,64,128]{2,1,0:T(8,128)S(1)}, f32[4,64,128]{2,1,0:T(8,128)}, u32[]{:S(2)}) copy-start(f32[4,64,128]{2,1,0:T(8,128)} %copy-done.7) | copy-start | bytes 393220
  80.8 13.6 %copy-start.11 = (f32[4,64,128]{2,1,0:T(8,128)S(1)}, f32[4,64,128]{2,1,0:T(8,128)}, u32[]{:S(2)}) copy-start(f32[4,64,128]{2,1,0:T(8,128)} %copy-done.10) | copy-start | bytes 393220
  80.8 13.6 %copy-start.14 = (f32[4,64,128]{2,1,0:T(8,128)S(1)}, f32[4,64,128]{2,1,0:T(8,128)}, u32[]{:S(2)}) copy-start(f32[4,64,128]{2,1,0:T(8,128)} %copy-done.13) | copy-start | bytes 393220
  80.8 13.6 %copy-start.17 = (f32[4,64,128]{2,1,0:T(8,128)S(1)}, f32[4,64,128]{2,1,0:T(8,128)}, u32[]{:S(2)}) copy-start(f32[4,64,128]{2,1,0:T(8,128)} %copy-done.16) | copy-start | bytes 393220
  80.8 13.6 %copy-start.20 = (f32[4,64,128]{2,1,0:T(8,128)S(1)}, f32[4,64,128]{2,1,0:T(8,128)}, u32[]{:S(2)}) copy-start(f32[4,64,128]{2,1,0:T(8,128)} %copy-done.19) | copy-start | bytes 393220
  80.8 13.6 %copy-start.23 = (f32[4,64,128]{2,1,0:T(8,128)S(1)}, f32[4,64,128]{2,1,0:T(8,128)}, u32[]{:S(2)}) copy-start(f32[4,64,128]{2,1,0:T(8,128)} %copy-done.22) | copy-start | bytes 393220
  80.8 13.6 %copy-start.34 = (f32[4,64,128]{2,1,0:T(8,128)S(1)}, f32[4,64,128]{2,1,0:T(8,128)}, u32[]{:S(2)}) copy-start(f32[4,64,128]{2,1,0:T(8,128)} %copy-done.33) | copy-start | bytes 393220
  80.8 13.6 %copy-start.37 = (f32[4,64,128]{2,1,0:T(8,128)S(1)}, f32[4,64,128]{2,1,0:T(8,128)}, u32[]{:S(2)}) copy-start(f32[4,64,128]{2,1,0:T(8,128)} %copy-done.36) | copy-start | bytes 393220
  80.8 13.6 %copy-start.40 = (f32[4,64,128]{2,1,0:T(8,128)S(1)}, f32[4,64,128]{2,1,0:T(8,128)}, u32[]{:S(2)}) copy-start(f32[4,64,128]{2,1,0:T(8,128)} %copy-done.39) | copy-start | bytes 393220
  100.7 37.8 %collective-permute-start.7 = (f32[9,1,64,128]{3,2,1,0:T(8,128)}, f32[9,1,64,128]{3,2,1,0:T(8,128)}, u32[]{:S(2)}, u32[]{:S(2)}) collective-permute-start(f32[9,1,64,128]{3,2,1,0:T(8,128)} %get-tuple-element.22), channel_id=1, source_target_pairs={{0,2},{2,4},{4,6},{6,8},{8,10},{10,12},{12,14},{14,16},{16,18},{18... | collective-permute-start | bytes 884744 | tf_op jit(solution)/shard_map/ppermute | solution.py:24
  105.0 33.4 %collective-permute-start.6 = (f32[9,1,64,128]{3,2,1,0:T(8,128)}, f32[9,1,64,128]{3,2,1,0:T(8,128)}, u32[]{:S(2)}, u32[]{:S(2)}) collective-permute-start(f32[9,1,64,128]{3,2,1,0:T(8,128)} %get-tuple-element.23), channel_id=1, source_target_pairs={{2,0},{4,2},{6,4},{8,6},{10,8},{12,10},{14,12},{16,14},{18,16},{20... | collective-permute-start | bytes 884744 | tf_op jit(solution)/shard_map/ppermute | solution.py:27
  138.3 4.1 %copy-start.18 = (f32[4,64,128]{2,1,0:T(8,128)S(1)}, f32[4,64,128]{2,1,0:T(8,128)}, u32[]{:S(2)}) copy-start(f32[4,64,128]{2,1,0:T(8,128)} %copy-done.16) | copy-start | bytes 393220
  138.3 4.1 %copy-start.21 = (f32[4,64,128]{2,1,0:T(8,128)S(1)}, f32[4,64,128]{2,1,0:T(8,128)}, u32[]{:S(2)}) copy-start(f32[4,64,128]{2,1,0:T(8,128)} %copy-done.19) | copy-start | bytes 393220
  138.4 4.1 %copy-start.24 = (f32[4,64,128]{2,1,0:T(8,128)S(1)}, f32[4,64,128]{2,1,0:T(8,128)}, u32[]{:S(2)}) copy-start(f32[4,64,128]{2,1,0:T(8,128)} %copy-done.22) | copy-start | bytes 393220
  138.4 4.1 %copy-start.26 = (f32[4,64,128]{2,1,0:T(8,128)S(1)}, f32[4,64,128]{2,1,0:T(8,128)}, u32[]{:S(2)}) copy-start(f32[4,64,128]{2,1,0:T(8,128)} %copy-done.25) | copy-start | bytes 393220
  138.4 4.1 %copy-start.28 = (f32[4,64,128]{2,1,0:T(8,128)S(1)}, f32[4,64,128]{2,1,0:T(8,128)}, u32[]{:S(2)}) copy-start(f32[4,64,128]{2,1,0:T(8,128)} %copy-done.27) | copy-start | bytes 393220
  138.4 4.1 %copy-start.30 = (f32[4,64,128]{2,1,0:T(8,128)S(1)}, f32[4,64,128]{2,1,0:T(8,128)}, u32[]{:S(2)}) copy-start(f32[4,64,128]{2,1,0:T(8,128)} %copy-done.29) | copy-start | bytes 393220
  138.4 4.1 %copy-start.32 = (f32[4,64,128]{2,1,0:T(8,128)S(1)}, f32[4,64,128]{2,1,0:T(8,128)}, u32[]{:S(2)}) copy-start(f32[4,64,128]{2,1,0:T(8,128)} %copy-done.31) | copy-start | bytes 393220
  138.4 4.1 %copy-start.35 = (f32[4,64,128]{2,1,0:T(8,128)S(1)}, f32[4,64,128]{2,1,0:T(8,128)}, u32[]{:S(2)}) copy-start(f32[4,64,128]{2,1,0:T(8,128)} %copy-done.33) | copy-start | bytes 393220
  148.8 8.8 %copy-start = (f32[8,4,64,128]{3,2,1,0:T(8,128)}, f32[8,4,64,128]{3,2,1,0:T(8,128)S(1)}, u32[]{:S(2)}) copy-start(f32[8,4,64,128]{3,2,1,0:T(8,128)S(1)} %fusion.84) | copy-start | bytes 3145732
  148.8 15.3 %copy-start.51 = (f32[128,8]{1,0:T(8,128)S(1)}, f32[128,8]{1,0:T(8,128)}, u32[]{:S(2)}) copy-start(f32[128,8]{1,0:T(8,128)} %gather_fusion) | copy-start | bytes 12292
  148.8 15.2 %copy-start.52 = (f32[128,8]{1,0:T(8,128)S(1)}, f32[128,8]{1,0:T(8,128)}, u32[]{:S(2)}) copy-start(f32[128,8]{1,0:T(8,128)} %gather_fusion.1) | copy-start | bytes 12292
  148.8 15.2 %copy-start.54 = (pred[128]{0:T(512)(128)(4,1)S(1)}, pred[128]{0:T(512)(128)(4,1)}, u32[]{:S(2)}) copy-start(pred[128]{0:T(512)(128)(4,1)} %get-tuple-element.8) | copy-start | bytes 388
  148.8 15.2 %copy-start.55 = (pred[128]{0:T(512)(128)(4,1)S(1)}, pred[128]{0:T(512)(128)(4,1)}, u32[]{:S(2)}) copy-start(pred[128]{0:T(512)(128)(4,1)} %get-tuple-element.56) | copy-start | bytes 388
  148.8 15.2 %copy-start.56 = (pred[128]{0:T(512)(128)(4,1)S(1)}, pred[128]{0:T(512)(128)(4,1)}, u32[]{:S(2)}) copy-start(pred[128]{0:T(512)(128)(4,1)} %get-tuple-element.55) | copy-start | bytes 388
  164.2 5.0 %collective-permute-start.8 = (f32[8,128]{0,1:T(8,128)S(1)}, f32[8,128]{0,1:T(8,128)S(1)}, u32[]{:S(2)}, u32[]{:S(2)}) collective-permute-start(f32[8,128]{0,1:T(8,128)S(1)} %fusion.108), channel_id=1, source_target_pairs={{0,2},{2,0},{4,6},{6,4},{8,10},{10,8},{12,14},{14,12},{16,18},{18,... | collective-permute-start | bytes 12296 | tf_op jit(solution)/shard_map/ppermute | solution.py:14
  169.2 4.3 %collective-permute-start.9 = (f32[8,128]{0,1:T(8,128)S(1)}, f32[8,128]{0,1:T(8,128)S(1)}, u32[]{:S(2)}, u32[]{:S(2)}) collective-permute-start(f32[8,128]{0,1:T(8,128)S(1)} %add.336), channel_id=1, source_target_pairs={{0,4},{2,6},{4,0},{6,2},{8,12},{10,14},{12,8},{14,10},{16,20},{18,... | collective-permute-start | bytes 12296 | tf_op jit(solution)/shard_map/ppermute | solution.py:14
  173.6 7.6 %collective-permute-start.10 = (f32[8,128]{0,1:T(8,128)S(1)}, f32[8,128]{0,1:T(8,128)S(1)}, u32[]{:S(2)}, u32[]{:S(2)}) collective-permute-start(f32[8,128]{0,1:T(8,128)S(1)} %add.337), channel_id=1, source_target_pairs={{0,8},{2,10},{4,12},{6,14},{8,0},{10,2},{12,4},{14,6},{16,24},{18,... | collective-permute-start | bytes 12296 | tf_op jit(solution)/shard_map/ppermute | solution.py:14
  181.1 5.2 %collective-permute-start.11 = (f32[8,128]{0,1:T(8,128)S(1)}, f32[8,128]{0,1:T(8,128)S(1)}, u32[]{:S(2)}, u32[]{:S(2)}) collective-permute-start(f32[8,128]{0,1:T(8,128)S(1)} %add.338), channel_id=1, source_target_pairs={{0,16},{2,18},{4,20},{6,22},{8,24},{10,26},{12,28},{14,30},{16,0},... | collective-permute-start | bytes 12296 | tf_op jit(solution)/shard_map/ppermute | solution.py:14
  (10 other events, 37.8 us)
Sparse Core Ops, SparseCore 0:
  25.5 20.9 all-reduce.6
